TPU v7x, 32 devices: a whole 2x2x4 slice. The times are simulated.
32 devices in a mesh: row: 32 (over z, y, x, core).
Axes of the slice: x: 2, y: 2, z: 4, core: 2. Of those that a mesh axis runs over, the one named last changes fastest.
Arguments:
- aux_slab: float32 [768, 16384], P(None, 'row'), may hold values from -0.21875 to 0.21875
- gaps: float32 [768], replicated, may hold values from 0.1 to 10
- frequency: float32 [1], replicated, may hold values from 0.1 to 10
Outputs:
- cyclic_matrix: float32 [32, 2048, 4096], P('row')
All inputs are finite; a program needn't handle non-finite values.
Results may differ from a plain program's by a relative error of at most 0.00005.
Values sent between devices are 32-bit elements; how exact they have to be, the bound alone decides.
A program may use at most 192 MiB of HBM per device.

v0:
```python
import jax
import jax.numpy as jnp
from jax import lax
from jax.sharding import PartitionSpec as P


def partner(value, axis, bit):
    return lax.ppermute(value, axis, [(i, i ^ 1 << bit) for i in range(lax.axis_size(axis))])


def gather_order(own_bit, mine_part, other_part):
    return jnp.where(
        own_bit == 1,
        jnp.concatenate([other_part, mine_part], 1),
        jnp.concatenate([mine_part, other_part], 1),
    )


def per_device(aux_slab, gaps, frequency):
    devices = lax.axis_size("row")
    bit_count = devices.bit_length() - 1
    low_bits = bit_count // 2
    high_bits = bit_count - low_bits
    grid_cols = 2**low_bits
    grid_rows = 2**high_bits
    position = lax.axis_index("row")
    width = aux_slab.shape[1]
    weights = 2.0 * gaps / (gaps * gaps + frequency[0] * frequency[0])
    weighted_panel = aux_slab * weights[:, None]
    for section_no in range(low_bits):
        received = partner(weighted_panel, "row", section_no)
        weighted_panel = gather_order(position >> section_no & 1, weighted_panel, received)
    column_panel = aux_slab
    for section_no in range(high_bits):
        dev_bit = low_bits + section_no
        received = partner(column_panel, "row", dev_bit)
        column_panel = gather_order(position >> dev_bit & 1, column_panel, received)
    product_tile = lax.dot_general(
        weighted_panel,
        column_panel,
        (((0,), (0,)), ((), ())),
        precision=lax.Precision.HIGHEST,
        preferred_element_type=jnp.float32,
    )
    tile_rows, tile_cols = product_tile.shape
    sections = [(level, level) for level in range(low_bits)]
    sections = sections + [(low_bits, 0)]
    blocks = product_tile.reshape(grid_cols, width, tile_cols)
    for dev_pos, slot_bit in sections:
        dev_bit = low_bits + dev_pos
        shaped = blocks.reshape(grid_cols // (2 * 2**slot_bit), 2, 2**slot_bit, width, tile_cols)
        own_bit = position >> dev_bit & 1
        kept_half = jnp.where(own_bit == 1, shaped[:, 1], shaped[:, 0])
        outgoing = jnp.where(own_bit == 1, shaped[:, 0], shaped[:, 1])
        received = partner(outgoing, "row", dev_bit)
        joined = jnp.where(
            own_bit == 1, jnp.stack([received, kept_half], 1), jnp.stack([kept_half, received], 1)
        )
        blocks = joined.reshape(grid_cols, width, tile_cols)
    blocks = blocks.reshape(grid_cols // 2, 2, width, tile_cols).transpose(1, 0, 2, 3)
    product_tile = blocks.reshape(tile_rows, tile_cols)
    grid_row = position >> low_bits
    grid_col = position & grid_cols - 1
    local_rows = jnp.arange(tile_rows, dtype=jnp.int32)
    local_cols = jnp.arange(tile_cols, dtype=jnp.int32)
    global_rows = (local_rows // width * grid_rows + grid_row) * width + local_rows % width
    global_cols = (local_cols // width * grid_cols + grid_col) * width + local_cols % width
    identity_part = (global_rows[:, None] == global_cols[None, :]).astype(jnp.float32)
    return (product_tile + identity_part)[None]


def solution(mesh):
    in_specs = (P(None, "row"), P(), P())
    out_specs = P("row", None, None)
    return jax.shard_map(
        per_device, mesh=mesh, in_specs=in_specs, out_specs=out_specs, check_vma=False
    )
```

profile of v0, /device:TPU:16, one launch (start us, length us, event | category | flops | bytes accessed | tf_op | source)
XLA Modules:
  0.0 2089.6 jit_solution(8982715092916361114)
XLA Ops:
  0.0 1.5 collective-permute-start.2
  1.5 34.9 %collective-permute-done.2 = f32[768,512]{1,0:T(8,128)} collective-permute-done((f32[768,512]{1,0:T(8,128)}, f32[768,512]{1,0:T(8,128)}, u32[]{:S(2)}, u32[]{:S(2)}) %collective-permute-start.2) | collective-permute-done | bytes 1572896 | tf_op jit(solution)/shard_map/ppermute | solution.py:8
  36.5 3.6 maximum_select_fusion.9
  40.0 1.6 collective-permute-start.3
  41.7 67.5 %collective-permute-done.3 = f32[768,1024]{1,0:T(8,128)} collective-permute-done((f32[768,1024]{1,0:T(8,128)S(1)}, f32[768,1024]{1,0:T(8,128)}, u32[]{:S(2)}, u32[]{:S(2)}) %collective-permute-start.3) | collective-permute-done | bytes 3145760 | tf_op jit(solution)/shard_map/ppermute | solution.py:8
  109.2 6.0 maximum_select_fusion.7
  115.2 0.4 collective-permute-start.4
  116.3 0.0 copy-done.1
  116.3 0.2 broadcast_multiply_fusion
  116.5 0.1 collective-permute-start
  116.6 3.4 collective-permute-done
  120.0 2.3 maximum_select_fusion.8
  122.3 1.4 collective-permute-start.1
  123.7 69.0 %collective-permute-done.1 = f32[768,1024]{1,0:T(8,128)S(1)} collective-permute-done((f32[768,1024]{1,0:T(8,128)}, f32[768,1024]{1,0:T(8,128)S(1)}, u32[]{:S(2)}, u32[]{:S(2)}) %collective-permute-start.1) | collective-permute-done | bytes 3145760 | tf_op jit(solution)/shard_map/ppermute | solution.py:8
  192.6 191.4 %collective-permute-done.4 = f32[768,2048]{1,0:T(8,128)} collective-permute-done((f32[768,2048]{1,0:T(8,128)}, f32[768,2048]{1,0:T(8,128)}, u32[]{:S(2)}, u32[]{:S(2)}) %collective-permute-start.4) | collective-permute-done | bytes 6291488 | tf_op jit(solution)/shard_map/ppermute | solution.py:8
  384.1 90.0 %fusion.3 = f32[2048,4096]{1,0:T(8,128)} fusion(f32[768,2048]{1,0:T(8,128)} %maximum_select_fusion.7, f32[768,2048]{1,0:T(8,128)} %collective-permute-done.4, f32[768,1024]{1,0:T(8,128)} %maximum_select_fusion.8, f32[768,1024]{1,0:T(8,128)S(1)} %collective-permute-done.1, pred[]{:T(512)S(6)} %eq.48, pred[]{:T(512)S(6)} %eq.51), kind=kOutput, calls=%fused_computation.14 | convolution fusion | flops 77323567104 | bytes 52428800 | tf_op jit(solution)/shard_map/dot_general | solution.py:38
  474.1 11.4 fusion.2
  485.4 1.2 collective-permute-start.5
  486.6 17.8 select_bitcast_fusion.2
  504.5 342.6 %collective-permute-done.5 = f32[2,1,512,4096]{3,2,0,1:T(8,128)} collective-permute-done((f32[2,1,512,4096]{3,2,0,1:T(8,128)S(1)}, f32[2,1,512,4096]{3,2,0,1:T(8,128)}, u32[]{:S(2)}, u32[]{:S(2)}) %collective-permute-start.5) | collective-permute-done | bytes 16777248 | tf_op jit(solution)/shard_map/ppermute | solution.py:8
  847.1 35.6 %maximum_select_fusion = f32[1,2,2,512,4096]{4,3,1,2,0:T(8,128)} fusion(f32[1,2,1,512,4096]{4,3,1,2,0:T(8,128)} %select_bitcast_fusion.2, f32[1,2,1,512,4096]{4,3,1,2,0:T(8,128)} %bitcast.4, pred[]{:T(512)S(6)} %eq.50), kind=kLoop, calls=%fused_computation | loop fusion | flops 25165824 | bytes 67108864 | tf_op jit(solution)/shard_map/jit(_where)/select_n | solution.py:56
  882.7 11.4 fusion.1
  894.1 4.8 collective-permute-start.6
  898.9 17.8 select_bitcast_fusion.1
  916.7 341.8 %collective-permute-done.6 = f32[1,2,512,4096]{3,2,1,0:T(8,128)} collective-permute-done((f32[1,2,512,4096]{3,2,1,0:T(8,128)S(1)}, f32[1,2,512,4096]{3,2,1,0:T(8,128)}, u32[]{:S(2)}, u32[]{:S(2)}) %collective-permute-start.6) | collective-permute-done | bytes 16777248 | tf_op jit(solution)/shard_map/ppermute | solution.py:8
  1258.6 35.6 %maximum_select_fusion.1 = f32[2,2,1,512,4096]{4,3,1,2,0:T(8,128)} fusion(f32[1,2,1,512,4096]{4,3,1,2,0:T(8,128)} %select_bitcast_fusion.1, f32[1,2,1,512,4096]{4,3,1,2,0:T(8,128)} %bitcast.10, pred[]{:T(512)S(6)} %eq.49), kind=kLoop, calls=%fused_computation.1 | loop fusion | flops 25165824 | bytes 67108864 | tf_op jit(solution)/shard_map/jit(_where)/select_n | solution.py:56
  1294.1 17.8 fusion
  1312.0 0.0 collective-permute-start.7
  1312.0 17.8 select_bitcast_fusion
  1329.8 700.4 %collective-permute-done.7 = f32[2,1,512,4096]{3,2,0,1:T(8,128)} collective-permute-done((f32[2,1,512,4096]{3,2,0,1:T(8,128)}, f32[2,1,512,4096]{3,2,0,1:T(8,128)}, u32[]{:S(2)}, u32[]{:S(2)}) %collective-permute-start.7) | collective-permute-done | bytes 16777248 | tf_op jit(solution)/shard_map/ppermute | solution.py:8
  2030.3 35.3 %maximum_select_fusion.2 = f32[2,2,512,4096]{3,2,0,1:T(8,128)} fusion(f32[2,1,512,4096]{3,2,0,1:T(8,128)} %select_bitcast_fusion, f32[2,1,512,4096]{3,2,0,1:T(8,128)} %collective-permute-done.7, pred[]{:T(512)S(6)} %eq.48), kind=kLoop, calls=%fused_computation.2 | loop fusion | flops 25165824 | bytes 67108864 | tf_op jit(solution)/shard_map/jit(_where)/select_n | solution.py:56
  2065.6 24.0 %convert_add_fusion = f32[1,2048,4096]{2,1,0:T(8,128)} fusion(f32[1,2048,4096]{2,1,0:T(8,128)} %bitcast.49, s32[4096]{0:T(1024)S(1)} %fusion.25, s32[2048]{0:T(1024)S(1)} %fusion.36), kind=kLoop, calls=%fused_computation.3 | loop fusion | flops 25165824 | bytes 67133440 | tf_op jit(solution)/shard_map/add | solution.py:69
  (6 shorter events, 0.0 us)
Async XLA Ops:
  0.0 116.3 %copy-start.1 = (f32[768]{0:T(1024)S(1)}, f32[768]{0:T(1024)}, u32[]{:S(2)}) copy-start(f32[768]{0:T(1024)} %param.4) | copy-start | bytes 9220
  0.0 36.5 %collective-permute-start.2 = (f32[768,512]{1,0:T(8,128)}, f32[768,512]{1,0:T(8,128)}, u32[]{:S(2)}, u32[]{:S(2)}) collective-permute-start(f32[768,512]{1,0:T(8,128)} %param.3), channel_id=1, source_target_pairs={{0,4},{1,5},{2,6},{3,7},{4,0},{5,1},{6,2},{7,3},{8,12},{9,13},{10,... | collective-permute-start | bytes 4718600 | tf_op jit(solution)/shard_map/ppermute | solution.py:8
  40.0 69.1 %collective-permute-start.3 = (f32[768,1024]{1,0:T(8,128)S(1)}, f32[768,1024]{1,0:T(8,128)}, u32[]{:S(2)}, u32[]{:S(2)}) collective-permute-start(f32[768,1024]{1,0:T(8,128)S(1)} %maximum_select_fusion.9), channel_id=1, source_target_pairs={{0,8},{1,9},{2,10},{3,11},{4,12},{5,13},{6,14},{7,15},{8,0},{9,1},... | collective-permute-start | bytes 9437192 | tf_op jit(solution)/shard_map/ppermute | solution.py:8
  41.7 74.6 %copy-start = (f32[768,512]{1,0:T(8,128)S(1)}, f32[768,512]{1,0:T(8,128)}, u32[]{:S(2)}) copy-start(f32[768,512]{1,0:T(8,128)} %param.3) | copy-start | bytes 4718596
  115.2 268.9 %collective-permute-start.4 = (f32[768,2048]{1,0:T(8,128)}, f32[768,2048]{1,0:T(8,128)}, u32[]{:S(2)}, u32[]{:S(2)}) collective-permute-start(f32[768,2048]{1,0:T(8,128)} %maximum_select_fusion.7), channel_id=1, source_target_pairs={{0,16},{1,17},{2,18},{3,19},{4,20},{5,21},{6,22},{7,23},{8,24},{9,... | collective-permute-start | bytes 18874376 | tf_op jit(solution)/shard_map/ppermute | solution.py:8
  116.5 3.5 collective-permute-start
  122.3 70.4 %collective-permute-start.1 = (f32[768,1024]{1,0:T(8,128)}, f32[768,1024]{1,0:T(8,128)S(1)}, u32[]{:S(2)}, u32[]{:S(2)}) collective-permute-start(f32[768,1024]{1,0:T(8,128)} %maximum_select_fusion.8), channel_id=1, source_target_pairs={{0,2},{1,3},{2,0},{3,1},{4,6},{5,7},{6,4},{7,5},{8,10},{9,11},{10,... | collective-permute-start | bytes 9437192 | tf_op jit(solution)/shard_map/ppermute | solution.py:8
  485.4 361.6 %collective-permute-start.5 = (f32[2,1,512,4096]{3,2,0,1:T(8,128)S(1)}, f32[2,1,512,4096]{3,2,0,1:T(8,128)}, u32[]{:S(2)}, u32[]{:S(2)}) collective-permute-start(f32[2,1,512,4096]{3,2,0,1:T(8,128)S(1)} %fusion.2), channel_id=1, source_target_pairs={{0,4},{1,5},{2,6},{3,7},{4,0},{5,1},{6,2},{7,3},{8,12},{9,13},{10,... | collective-permute-start | bytes 50331656 | tf_op jit(solution)/shard_map/ppermute | solution.py:8
  894.1 364.5 %collective-permute-start.6 = (f32[1,2,512,4096]{3,2,1,0:T(8,128)S(1)}, f32[1,2,512,4096]{3,2,1,0:T(8,128)}, u32[]{:S(2)}, u32[]{:S(2)}) collective-permute-start(f32[1,2,512,4096]{3,2,1,0:T(8,128)S(1)} %fusion.1), channel_id=1, source_target_pairs={{0,8},{1,9},{2,10},{3,11},{4,12},{5,13},{6,14},{7,15},{8,0},{9,1},... | collective-permute-start | bytes 50331656 | tf_op jit(solution)/shard_map/ppermute | solution.py:8
  1312.0 718.3 %collective-permute-start.7 = (f32[2,1,512,4096]{3,2,0,1:T(8,128)}, f32[2,1,512,4096]{3,2,0,1:T(8,128)}, u32[]{:S(2)}, u32[]{:S(2)}) collective-permute-start(f32[2,1,512,4096]{3,2,0,1:T(8,128)} %fusion), channel_id=1, source_target_pairs={{0,16},{1,17},{2,18},{3,19},{4,20},{5,21},{6,22},{7,23},{8,24},{9,... | collective-permute-start | bytes 50331656 | tf_op jit(solution)/shard_map/ppermute | solution.py:8
where the time goes:
time: 2090 us
  waiting for transfers between devices  1750 us (84%)
  other arithmetic  237 us (11%)
  matrix products  90 us (4%)
    ppermute x8, waiting for transfers between devices, partner(): lax.ppermute(value, axis, [(i, i ^ 1 << bit) for i in range(lax.axis_size...  1750 us
    select_n x3, other arithmetic, per_device(): jnp.where(own_bit == 1, jnp.stack([received, kept_half], 1), jnp.stack([k...  107 us
    dot_general x1, matrix products, per_device(): lax.dot_general(weighted_panel, column_panel, (((0,), (0,)), ((), ())), p...  90 us
    another operation x3, other arithmetic, per_device(): jnp.stack([received, kept_half], 1)  53.5 us
  transfers between devices with their start and end apart: 8, of which 8 were waited for; matrix products, arithmetic and copies ran while one was open for 3% of the time, Pallas kernels for 0%

commit v1 on v0

v1 whole, which is shorter than its diff:
```python
import functools
import jax
import jax.numpy as jnp
from jax import lax
from jax.experimental import pallas as pl
from jax.experimental.pallas import tpu as pltpu
from jax.sharding import PartitionSpec as P

MESH = pl.DeviceIdType.MESH
CHUNKS = 4
LAG = 2


def slot_at(place, grid_rows):
    place = lax.rem(place + 2 * grid_rows, grid_rows)
    return jnp.where(place < grid_rows // 2, 2 * place, 2 * (grid_rows - 1 - place) + 1)


def place_of(slot, grid_rows):
    return jnp.where(lax.rem(slot, 2) == 0, slot // 2, grid_rows - 1 - slot // 2)


def flipped(value, weight):
    return value + weight * (1 - 2 * lax.rem(value // weight, 2))


def gather_kernel(
    grid_rows, grid_cols, block_ref, col_ref, row_ref, own_sem, keep_sem, ring_send, ring_recv, row_send, row_recv
):
    bits = grid_cols.bit_length() - 1
    half = grid_rows // 2
    depth = block_ref.shape[0] // CHUNKS
    spread = grid_rows // grid_cols
    me = lax.axis_index("row")
    grid_row, grid_col = me // grid_cols, lax.rem(me, grid_cols)
    source_col = lax.rem(grid_row, grid_cols)
    place = place_of(grid_row, grid_rows)
    right = slot_at(place + 1, grid_rows) * grid_cols + grid_col
    left = slot_at(place - 1, grid_rows) * grid_cols + grid_col
    neighbours = (right, left)
    differs = [
        lax.rem(grid_col // 2**bit + source_col // 2**bit, 2) for bit in range(bits)
    ]
    none_below = [jnp.int32(1)]
    for bit in range(bits):
        none_below.append(none_below[-1] * (1 - differs[bit]))
    is_source = none_below[bits] == 1
    passes = [none_below[bit + 1] == 1 for bit in range(bits)]
    children = [grid_row * grid_cols + flipped(grid_col, 2**bit) for bit in range(bits)]

    own_copy = pltpu.make_async_copy(block_ref, col_ref.at[grid_row], own_sem)
    own_copy.start()
    barrier = pltpu.get_barrier_semaphore()
    for dev in (right, left):
        pl.semaphore_signal(barrier, inc=1, device_id=(dev,), device_id_type=MESH)
    for step in range(1, grid_cols):
        dev = grid_row * grid_cols + lax.rem(grid_col + step, grid_cols)
        pl.semaphore_signal(barrier, inc=1, device_id=(dev,), device_id_type=MESH)
    pl.semaphore_wait(barrier, 1 + grid_cols)
    own_copy.wait()

    def chunk(ref, slot, part):
        return ref.at[slot, pl.ds(pl.multiple_of(part * depth, 8), depth), :]

    def ring_copy(way, slot, step, part):
        return pltpu.make_async_remote_copy(
            src_ref=chunk(col_ref, slot, part),
            dst_ref=chunk(col_ref, slot, part),
            send_sem=ring_send.at[way, step, part],
            recv_sem=ring_recv.at[way, step, part],
            device_id=(neighbours[way],),
            device_id_type=MESH,
        )

    def row_copy(ref, slot, row_slot, part, bit):
        return pltpu.make_async_remote_copy(
            src_ref=chunk(ref, slot, part),
            dst_ref=chunk(row_ref, row_slot, part),
            send_sem=row_send.at[bit, row_slot, part],
            recv_sem=row_recv.at[row_slot, part],
            device_id=(children[bit],),
            device_id_type=MESH,
        )

    def keep_copy(slot, row_slot, part):
        return pltpu.make_async_copy(
            chunk(col_ref, slot, part), chunk(row_ref, row_slot, part), keep_sem.at[row_slot, part]
        )

    def event(index):
        step, turn = index // CHUNKS, lax.rem(index, CHUNKS)
        ways = []
        for way, part in ((0, turn), (1, CHUNKS - 1 - turn)):
            slot = slot_at(place - step if way == 0 else place + step, grid_rows)
            sends = (step < half - 1) | ((step == half - 1) & (turn < CHUNKS // 2))
            counts = (step > 0) if way == 1 else (step >= 0)
            in_row = counts & (lax.rem(slot, spread) == grid_row // grid_cols)
            ways.append((way, part, slot, slot // spread, step, sends, in_row))
        return ways

    total = half * CHUNKS + CHUNKS // 2

    def arrive(index):
        for way, part, slot, row_slot, step, sends, in_row in event(index):

            @pl.when(step > 0)
            def _():
                ring_copy(way, slot, step - 1, part).wait_recv()

            @pl.when(sends)
            def _():
                ring_copy(way, slot, step, part).start()

            @pl.when(in_row & is_source)
            def _():
                for bit in range(bits - 1, -1, -1):
                    row_copy(col_ref, slot, row_slot, part, bit).start()
                keep_copy(slot, row_slot, part).start()

    def relay(index):
        for way, part, slot, row_slot, step, sends, in_row in event(index):

            @pl.when(in_row & jnp.logical_not(is_source))
            def _():
                row_copy(col_ref, slot, row_slot, part, 0).wait_recv()
                for bit in range(bits - 1, -1, -1):

                    @pl.when(passes[bit])
                    def _():
                        row_copy(row_ref, row_slot, row_slot, part, bit).start()

    def drain(index):
        for way, part, slot, row_slot, step, sends, in_row in event(index):

            @pl.when(sends)
            def _():
                ring_copy(way, slot, step, part).wait_send()

            for bit in range(bits):

                @pl.when(in_row & passes[bit])
                def _():
                    row_copy(col_ref, slot, row_slot, part, bit).wait_send()

            @pl.when(in_row & is_source)
            def _():
                keep_copy(slot, row_slot, part).wait()

    @pl.loop(0, total + LAG)
    def _(index):
        @pl.when(index < total)
        def _():
            arrive(index)

        @pl.when(index >= LAG)
        def _():
            relay(index - LAG)

    @pl.loop(0, total)
    def _(index):
        drain(index)


def gather_panels(block, grid_rows, grid_cols):
    bits = grid_cols.bit_length() - 1
    half = grid_rows // 2
    return pl.pallas_call(
        functools.partial(gather_kernel, grid_rows, grid_cols),
        out_shape=[
            jax.ShapeDtypeStruct((grid_rows, *block.shape), jnp.float32),
            jax.ShapeDtypeStruct((grid_cols, *block.shape), jnp.float32),
        ],
        in_specs=[pl.BlockSpec(memory_space=pl.ANY)],
        out_specs=[pl.BlockSpec(memory_space=pl.ANY)] * 2,
        scratch_shapes=[
            pltpu.SemaphoreType.DMA,
            pltpu.SemaphoreType.DMA((grid_cols, CHUNKS)),
            pltpu.SemaphoreType.DMA((2, half, CHUNKS)),
            pltpu.SemaphoreType.DMA((2, half, CHUNKS)),
            pltpu.SemaphoreType.DMA((bits, grid_cols, CHUNKS)),
            pltpu.SemaphoreType.DMA((grid_cols, CHUNKS)),
        ],
        compiler_params=pltpu.CompilerParams(collective_id=0, has_side_effects=True),
        name="gather_panels",
    )(block)


def split(value):
    high = value.astype(jnp.bfloat16)
    return high, (value - high.astype(jnp.float32)).astype(jnp.bfloat16)


def product_kernel(grid_rows, grid_cols, row_ref, col_ref, out_ref, row_high, row_low, col_high, col_low):
    u, v = pl.program_id(0), pl.program_id(1)
    me = lax.axis_index("row")
    grid_row, grid_col = me // grid_cols, lax.rem(me, grid_cols)

    @pl.when(v == 0)
    def _():
        high, low = split(row_ref[0].T)
        row_high[...] = high
        row_low[...] = low

    @pl.when(u == 0)
    def _():
        high, low = split(col_ref[0])
        col_high[v] = high
        col_low[v] = low

    def dot(left, right):
        return jnp.dot(left[...], right, preferred_element_type=jnp.float32)

    out_ref[...] = dot(row_high, col_high[v]) + (dot(row_high, col_low[v]) + dot(row_low, col_high[v]))

    @pl.when(u * grid_rows + grid_row == v * grid_cols + grid_col)
    def _():
        width = out_ref.shape[0]
        lines = lax.broadcasted_iota(jnp.int32, (width, width), 0)
        lanes = lax.broadcasted_iota(jnp.int32, (width, width), 1)
        out_ref[...] += (lines == lanes).astype(jnp.float32)


def product(row_panel, col_panel):
    grid_cols, rows, width = row_panel.shape
    grid_rows = col_panel.shape[0]
    return pl.pallas_call(
        functools.partial(product_kernel, grid_rows, grid_cols),
        grid=(grid_cols, grid_rows),
        in_specs=[
            pl.BlockSpec((1, rows, width), lambda u, v: (u, 0, 0)),
            pl.BlockSpec((1, rows, width), lambda u, v: (jnp.where(u == 0, v, grid_rows - 1), 0, 0)),
        ],
        out_specs=pl.BlockSpec((width, width), lambda u, v: (u, v)),
        out_shape=jax.ShapeDtypeStruct((grid_cols * width, grid_rows * width), jnp.float32),
        scratch_shapes=[
            pltpu.VMEM((width, rows), jnp.bfloat16),
            pltpu.VMEM((width, rows), jnp.bfloat16),
            pltpu.VMEM((grid_rows, rows, width), jnp.bfloat16),
            pltpu.VMEM((grid_rows, rows, width), jnp.bfloat16),
        ],
        compiler_params=pltpu.CompilerParams(vmem_limit_bytes=48 * 2**20),
        name="product",
    )(row_panel, col_panel)


def per_device(aux_slab, gaps, frequency):
    devices = lax.axis_size("row")
    bit_count = devices.bit_length() - 1
    grid_cols = 2 ** (bit_count // 2)
    grid_rows = devices // grid_cols
    weights = 2.0 * gaps / (gaps * gaps + frequency[0] * frequency[0])
    block = aux_slab * jnp.sqrt(weights)[:, None]
    col_panel, row_panel = gather_panels(block, grid_rows, grid_cols)
    return product(row_panel, col_panel)[None]


def solution(mesh):
    in_specs = (P(None, "row"), P(), P())
    out_specs = P("row", None, None)
    return jax.shard_map(
        per_device, mesh=mesh, in_specs=in_specs, out_specs=out_specs, check_vma=False
    )
```

time: 2090 us -> 345 us (0.17)
  waiting for transfers between devices: 1750 us -> 0 us
  Pallas kernels: 0 us -> 341 us
  other arithmetic: 237 us -> 3.43 us
  matrix products: 90 us -> 0 us
    ppermute x8 -> x0, waiting for transfers between devices: 1750 us -> none  [partner(): lax.ppermute(value, axis, [(i, i ^ 1 << bit) for i in range(lax.axis_size...]
    pallas_call x0 -> x2, Pallas kernels: none -> 341 us  [the longest x1 287 us: gather_panels(): pl.pallas_call(functools.partial(gather_kernel, grid_rows, grid_cols), ou...]
    select_n x9 -> x0, other arithmetic: 159 us -> none  [the longest x3 107 us: per_device(): jnp.where(own_bit == 1, jnp.stack([received, kept_half], 1), jnp.stack([k...]
    dot_general x1 -> x0, matrix products: 90 us -> none  [per_device(): lax.dot_general(weighted_panel, column_panel, (((0,), (0,)), ((), ())), p...]
    another operation x3 -> x0, other arithmetic: 53.5 us -> none  [per_device(): jnp.stack([received, kept_half], 1)]
    add x3 -> x0, other arithmetic: 24 us -> none  [the longest x1 24 us: per_device(): return (product_tile + identity_part)[None]]
  transfers between devices with their start and end apart: 8 -> 0, of which waited for: 8 -> 0; matrix products, arithmetic and copies ran while one was open for 3% -> 0% of each run, Pallas kernels for 0% -> 0%
where the time goes in v1:
time: 345 us
  Pallas kernels  341 us (99%)
    pallas_call x1, Pallas kernels, gather_panels(): pl.pallas_call(functools.partial(gather_kernel, grid_rows, grid_cols), ou...  287 us
    pallas_call x1, Pallas kernels, product(): pl.pallas_call(functools.partial(product_kernel, grid_rows, grid_cols), g...  53.5 us

profile of v1, /device:TPU:16, one launch (start us, length us, event | category | flops | bytes accessed | tf_op | source)
XLA Modules:
  0.0 344.7 jit_solution(8490581605977452320)
XLA Ops:
  0.7 0.7 divide_sqrt_fusion
  1.4 2.7 broadcast_multiply_fusion.block_ref
  4.1 287.1 %gather_panels.1 = (f32[8,768,512]{2,1,0:T(8,128)}, f32[4,768,512]{2,1,0:T(8,128)}) custom-call(f32[768,512]{1,0:T(8,128)} %broadcast_multiply_fusion.block_ref), custom_call_target="tpu_custom_call" | custom-call | tf_op jit(solution)/shard_map/gather_panels/pallas_call | solution.py:167
  291.2 53.5 %product.1 = f32[2048,4096]{1,0:T(8,128)} custom-call(f32[4,768,512]{2,1,0:T(8,128)} %get-tuple-element.7.row_ref, f32[8,768,512]{2,1,0:T(8,128)} %get-tuple-element.8.col_ref), custom_call_target="tpu_custom_call" | custom-call | tf_op jit(solution)/shard_map/product/pallas_call | solution.py:226

commit v2 on v1

--- a/solution.py
+++ b/solution.py
@@ -24,12 +24,14 @@
     return value + weight * (1 - 2 * lax.rem(value // weight, 2))
 
 
-def gather_kernel(
-    grid_rows, grid_cols, block_ref, col_ref, row_ref, own_sem, keep_sem, ring_send, ring_recv, row_send, row_recv
+def coupling_kernel(
+    grid_rows, grid_cols, block_ref, scale_ref, out_ref, col_ref, row_ref, row_high, row_low, col_high, col_low,
+    tile_ref, own_sem, tile_sem, ring_send, ring_recv, row_send, row_recv
 ):
     bits = grid_cols.bit_length() - 1
     half = grid_rows // 2
     depth = block_ref.shape[0] // CHUNKS
+    width = block_ref.shape[1]
     spread = grid_rows // grid_cols
     me = lax.axis_index("row")
     grid_row, grid_col = me // grid_cols, lax.rem(me, grid_cols)
@@ -56,8 +58,9 @@
     for step in range(1, grid_cols):
         dev = grid_row * grid_cols + lax.rem(grid_col + step, grid_cols)
         pl.semaphore_signal(barrier, inc=1, device_id=(dev,), device_id_type=MESH)
+    own_copy.wait()
+    col_ref[grid_row] = col_ref[grid_row] * scale_ref[...]
     pl.semaphore_wait(barrier, 1 + grid_cols)
-    own_copy.wait()
 
     def chunk(ref, slot, part):
         return ref.at[slot, pl.ds(pl.multiple_of(part * depth, 8), depth), :]
@@ -80,11 +83,6 @@
             recv_sem=row_recv.at[row_slot, part],
             device_id=(children[bit],),
             device_id_type=MESH,
-        )
-
-    def keep_copy(slot, row_slot, part):
-        return pltpu.make_async_copy(
-            chunk(col_ref, slot, part), chunk(row_ref, row_slot, part), keep_sem.at[row_slot, part]
         )
 
     def event(index):
@@ -115,7 +113,6 @@
             def _():
                 for bit in range(bits - 1, -1, -1):
                     row_copy(col_ref, slot, row_slot, part, bit).start()
-                keep_copy(slot, row_slot, part).start()
 
     def relay(index):
         for way, part, slot, row_slot, step, sends, in_row in event(index):
@@ -142,105 +139,144 @@
                 def _():
                     row_copy(col_ref, slot, row_slot, part, bit).wait_send()
 
-            @pl.when(in_row & is_source)
-            def _():
-                keep_copy(slot, row_slot, part).wait()
-
-    @pl.loop(0, total + LAG)
-    def _(index):
+    def distance(slot):
+        ahead = lax.rem(place_of(slot, grid_rows) - place + grid_rows, grid_rows)
+        return jnp.minimum(ahead, grid_rows - ahead)
+
+    def row_origin(u):
+        return u * spread + grid_row // grid_cols
+
+    def prepare_row(u, ref, slot):
+        high, low = split(ref[slot].T)
+        row_high[u] = high
+        row_low[u] = low
+
+    def prepare(level):
+        @pl.loop(0, grid_rows)
+        def _(v):
+            @pl.when(distance(v) == level)
+            def _():
+                high, low = split(col_ref[v])
+                col_high[v] = high
+                col_low[v] = low
+
+        @pl.loop(0, grid_cols)
+        def _(u):
+            new = distance(row_origin(u)) == level
+
+            @pl.when(new & is_source)
+            def _():
+                prepare_row(u, col_ref, row_origin(u))
+
+            @pl.when(new & jnp.logical_not(is_source))
+            def _():
+                prepare_row(u, row_ref, u)
+
+    def tile_copy(u, v, buffer):
+        return pltpu.make_async_copy(
+            tile_ref.at[buffer],
+            out_ref.at[
+                pl.ds(pl.multiple_of(u * width, width), width), pl.ds(pl.multiple_of(v * width, width), width)
+            ],
+            tile_sem.at[buffer],
+        )
+
+    def dot(first, second):
+        return jnp.dot(first, second, preferred_element_type=jnp.float32)
+
+    def multiply(level, turn, count):
+        def pair(number, count):
+            u, v = number // grid_rows, lax.rem(number, grid_rows)
+            due = jnp.maximum(distance(v), distance(row_origin(u))) == level
+            due = due & (lax.rem(u + v, CHUNKS) == turn)
+            buffer = lax.rem(count, 2)
+
+            @pl.when(due)
+            def _():
+                @pl.when(count >= 2)
+                def _():
+                    tile_copy(u, v, buffer).wait()
+
+                high = row_high[u]
+                tile_ref[buffer] = dot(high, col_high[v]) + (dot(high, col_low[v]) + dot(row_low[u], col_high[v]))
+
+                @pl.when(u * grid_rows + grid_row == v * grid_cols + grid_col)
+                def _():
+                    lines = lax.broadcasted_iota(jnp.int32, (width, width), 0)
+                    lanes = lax.broadcasted_iota(jnp.int32, (width, width), 1)
+                    tile_ref[buffer] += (lines == lanes).astype(jnp.float32)
+
+                tile_copy(u, v, buffer).start()
+
+            return count + due.astype(jnp.int32)
+
+        return lax.fori_loop(0, grid_cols * grid_rows, pair, count)
+
+    wait_levels = LAG + CHUNKS - 1
+
+    def body(index, count):
         @pl.when(index < total)
         def _():
             arrive(index)
 
-        @pl.when(index >= LAG)
+        @pl.when((index >= LAG) & (index < total + LAG))
         def _():
             relay(index - LAG)
+
+        ready = index >= wait_levels
+        level = jnp.where(ready, (index - wait_levels) // CHUNKS, -1)
+        turn = lax.rem(index + CHUNKS * wait_levels - wait_levels, CHUNKS)
+
+        @pl.when(ready & (turn == 0))
+        def _():
+            prepare(level)
+
+        return multiply(level, turn, count)
+
+    lax.fori_loop(0, wait_levels + (half + 1) * CHUNKS, body, jnp.int32(0))
+
+    for buffer in range(2):
+        tile_copy(0, 0, buffer).wait()
 
     @pl.loop(0, total)
     def _(index):
         drain(index)
 
 
-def gather_panels(block, grid_rows, grid_cols):
+def split(value):
+    high = value.astype(jnp.bfloat16)
+    return high, (value - high.astype(jnp.float32)).astype(jnp.bfloat16)
+
+
+def coupling_tile(block, scale, grid_rows, grid_cols):
     bits = grid_cols.bit_length() - 1
     half = grid_rows // 2
+    rows, width = block.shape
     return pl.pallas_call(
-        functools.partial(gather_kernel, grid_rows, grid_cols),
-        out_shape=[
-            jax.ShapeDtypeStruct((grid_rows, *block.shape), jnp.float32),
-            jax.ShapeDtypeStruct((grid_cols, *block.shape), jnp.float32),
-        ],
-        in_specs=[pl.BlockSpec(memory_space=pl.ANY)],
-        out_specs=[pl.BlockSpec(memory_space=pl.ANY)] * 2,
+        functools.partial(coupling_kernel, grid_rows, grid_cols),
+        out_shape=jax.ShapeDtypeStruct((grid_cols * width, grid_rows * width), jnp.float32),
+        in_specs=[pl.BlockSpec(memory_space=pl.ANY), pl.BlockSpec(memory_space=pltpu.VMEM)],
+        out_specs=pl.BlockSpec(memory_space=pl.ANY),
         scratch_shapes=[
+            pltpu.VMEM((grid_rows, rows, width), jnp.float32),
+            pltpu.VMEM((grid_cols, rows, width), jnp.float32),
+            pltpu.VMEM((grid_cols, width, rows), jnp.bfloat16),
+            pltpu.VMEM((grid_cols, width, rows), jnp.bfloat16),
+            pltpu.VMEM((grid_rows, rows, width), jnp.bfloat16),
+            pltpu.VMEM((grid_rows, rows, width), jnp.bfloat16),
+            pltpu.VMEM((2, width, width), jnp.float32),
             pltpu.SemaphoreType.DMA,
-            pltpu.SemaphoreType.DMA((grid_cols, CHUNKS)),
+            pltpu.SemaphoreType.DMA((2,)),
             pltpu.SemaphoreType.DMA((2, half, CHUNKS)),
             pltpu.SemaphoreType.DMA((2, half, CHUNKS)),
             pltpu.SemaphoreType.DMA((bits, grid_cols, CHUNKS)),
             pltpu.SemaphoreType.DMA((grid_cols, CHUNKS)),
         ],
-        compiler_params=pltpu.CompilerParams(collective_id=0, has_side_effects=True),
-        name="gather_panels",
-    )(block)
-
-
-def split(value):
-    high = value.astype(jnp.bfloat16)
-    return high, (value - high.astype(jnp.float32)).astype(jnp.bfloat16)
-
-
-def product_kernel(grid_rows, grid_cols, row_ref, col_ref, out_ref, row_high, row_low, col_high, col_low):
-    u, v = pl.program_id(0), pl.program_id(1)
-    me = lax.axis_index("row")
-    grid_row, grid_col = me // grid_cols, lax.rem(me, grid_cols)
-
-    @pl.when(v == 0)
-    def _():
-        high, low = split(row_ref[0].T)
-        row_high[...] = high
-        row_low[...] = low
-
-    @pl.when(u == 0)
-    def _():
-        high, low = split(col_ref[0])
-        col_high[v] = high
-        col_low[v] = low
-
-    def dot(left, right):
-        return jnp.dot(left[...], right, preferred_element_type=jnp.float32)
-
-    out_ref[...] = dot(row_high, col_high[v]) + (dot(row_high, col_low[v]) + dot(row_low, col_high[v]))
-
-    @pl.when(u * grid_rows + grid_row == v * grid_cols + grid_col)
-    def _():
-        width = out_ref.shape[0]
-        lines = lax.broadcasted_iota(jnp.int32, (width, width), 0)
-        lanes = lax.broadcasted_iota(jnp.int32, (width, width), 1)
-        out_ref[...] += (lines == lanes).astype(jnp.float32)
-
-
-def product(row_panel, col_panel):
-    grid_cols, rows, width = row_panel.shape
-    grid_rows = col_panel.shape[0]
-    return pl.pallas_call(
-        functools.partial(product_kernel, grid_rows, grid_cols),
-        grid=(grid_cols, grid_rows),
-        in_specs=[
-            pl.BlockSpec((1, rows, width), lambda u, v: (u, 0, 0)),
-            pl.BlockSpec((1, rows, width), lambda u, v: (jnp.where(u == 0, v, grid_rows - 1), 0, 0)),
-        ],
-        out_specs=pl.BlockSpec((width, width), lambda u, v: (u, v)),
-        out_shape=jax.ShapeDtypeStruct((grid_cols * width, grid_rows * width), jnp.float32),
-        scratch_shapes=[
-            pltpu.VMEM((width, rows), jnp.bfloat16),
-            pltpu.VMEM((width, rows), jnp.bfloat16),
-            pltpu.VMEM((grid_rows, rows, width), jnp.bfloat16),
-            pltpu.VMEM((grid_rows, rows, width), jnp.bfloat16),
-        ],
-        compiler_params=pltpu.CompilerParams(vmem_limit_bytes=48 * 2**20),
-        name="product",
-    )(row_panel, col_panel)
+        compiler_params=pltpu.CompilerParams(
+            collective_id=0, has_side_effects=True, vmem_limit_bytes=56 * 2**20
+        ),
+        name="coupling_tile",
+    )(block, scale)
 
 
 def per_device(aux_slab, gaps, frequency):
@@ -249,9 +285,7 @@
     grid_cols = 2 ** (bit_count // 2)
     grid_rows = devices // grid_cols
     weights = 2.0 * gaps / (gaps * gaps + frequency[0] * frequency[0])
-    block = aux_slab * jnp.sqrt(weights)[:, None]
-    col_panel, row_panel = gather_panels(block, grid_rows, grid_cols)
-    return product(row_panel, col_panel)[None]
+    return coupling_tile(aux_slab, jnp.sqrt(weights)[:, None], grid_rows, grid_cols)[None]
 
 
 def solution(mesh):

time: 345 us -> 204 us (0.59)
  Pallas kernels: 341 us -> 176 us
  local copies, waits for them, and re-layouts: 0 us -> 23.9 us
    pallas_call x2 -> x1, Pallas kernels: 341 us -> 176 us  [coupling_tile(): pl.pallas_call(functools.partial(coupling_kernel, grid_rows, grid_cols),...]
    unnamed x0 -> x1, local copies, waits for them, and re-layouts: none -> 23 us
where the time goes in v2:
time: 204 us; the launch traced here: 201 us
  Pallas kernels  176 us (86%)
  local copies, waits for them, and re-layouts  23.9 us (12%)
    pallas_call x1, Pallas kernels, coupling_tile(): pl.pallas_call(functools.partial(coupling_kernel, grid_rows, grid_cols),...  176 us
    unnamed x1, local copies, waits for them, and re-layouts  23 us

profile of v2, /device:TPU:16, one launch (start us, length us, event | category | flops | bytes accessed | tf_op | source)
XLA Modules:
  0.0 201.4 jit_solution(10324642703613507296)
XLA Ops:
  0.7 0.7 divide_sqrt_fusion
  1.4 0.9 broadcast_in_dim.8.scale_ref
  2.3 176.1 %coupling_tile.1 = f32[2048,4096]{1,0:T(8,128)} custom-call(f32[768,512]{1,0:T(8,128)} %block_ref.1, f32[768,1]{1,0:T(8,128)} %broadcast_in_dim.8.scale_ref), custom_call_target="tpu_custom_call" | custom-call | tf_op jit(solution)/shard_map/coupling_tile/pallas_call | solution.py:255
  178.4 23.0 %copy.7 = f32[1,2048,4096]{2,1,0:T(8,128)} copy(f32[1,2048,4096]{2,1,0:T(8,128)} %bitcast.2) | data formatting | bytes 67108864
